TPU v7x, 256 devices: a whole 4x4x8 slice. The times are simulated.
256 devices in a mesh: cls: 8 (over x_lo, y), dom: 32 (over x_hi, z, core).
Axes of the slice: x: 4 (x_hi: 2, x_lo: 2; x = x_hi * 2 + x_lo), y: 4, z: 8, core: 2. Of those that a mesh axis runs over, the one named last changes fastest.
Arguments:
- particles: bfloat16 [8192, 32768], P(('cls', 'dom')), may hold values from -16 to 16
- references: bfloat16 [16, 8, 32768], P('cls'), may hold values from -4 to 4
- orient_bins: int32 [8192], P(('cls', 'dom')), may hold values from 0 to 7
- destinations: int32 [8192, 1], P(('cls', 'dom')), may hold values from 0 to 31; in each aligned block of 32 rows (0 to 31, 32 to 63, ...) at most 2 rows name the same one
- group_slots: int32 [8192], P(('cls', 'dom')), may hold values from 0 to 7
Outputs:
- class_means: float32 [16, 8, 32768], P('cls', None, 'dom')
Inputs may be any that keep to these rules, and one draw needn't show every extreme that they name: `destinations`: among the rows of one device at most 2 name the same destination.
All inputs are finite; a program needn't handle non-finite values.
Results may differ from a plain program's by a relative error of at most 0.0047.
Values may be sent and summed in bfloat16 or wider, within the bound.
A program may use at most 128 MiB of HBM per device.

v0:
```python
import math

import jax
import jax.numpy as jnp
from jax import lax
from jax.sharding import PartitionSpec as P


def shards(particles, references, orient_bins, destinations, group_slots):
    sources = lax.axis_size("dom")
    row_count = particles.shape[0]
    voxels = particles.shape[1]
    capacity = max(2, (3 * row_count + 2 * sources - 1) // (2 * sources))
    groups = max(8, capacity)
    block_classes = references.shape[0]
    bins_all = references.shape[1]
    classes = block_classes * lax.axis_size("cls")
    slot_count = sources * capacity
    target = destinations[:, 0]
    target_hot = (target[:, None] == jnp.arange(sources, dtype=jnp.int32)[None, :]).astype(
        jnp.int32
    )
    position = jnp.sum((jnp.cumsum(target_hot, axis=0) - 1) * target_hot, axis=1)
    slot_index = target * capacity + position
    placement_map = jnp.arange(slot_count, dtype=jnp.int32)[:, None] == slot_index[None, :]
    outgoing = jnp.dot(
        placement_map.astype(jnp.bfloat16), particles, preferred_element_type=jnp.float32
    ).astype(jnp.bfloat16)
    labels = (1 + group_slots + groups * orient_bins).astype(jnp.float32)
    outgoing_codes = jnp.sum(jnp.where(placement_map, labels[None, :], 0.0), axis=1).astype(
        jnp.bfloat16
    )
    arrived, arrived_codes = (
        lax.all_to_all(
            outgoing.reshape(sources, capacity, voxels),
            "dom",
            split_axis=0,
            concat_axis=0,
            tiled=True,
        ),
        lax.all_to_all(
            outgoing_codes.reshape(sources, capacity),
            "dom",
            split_axis=0,
            concat_axis=0,
            tiled=True,
        ),
    )
    subvolumes = arrived.reshape(slot_count, voxels)
    slot_codes = arrived_codes.reshape(slot_count).astype(jnp.float32).astype(jnp.int32) - 1
    occupied = slot_codes >= 0
    member = jnp.where(occupied, slot_codes % groups, 0)
    orient = jnp.where(occupied, slot_codes // groups, -1)
    member_hot = (
        (member[:, None] == jnp.arange(groups, dtype=jnp.int32)[None, :]) & occupied[:, None]
    ).astype(jnp.float32)
    values = subvolumes.astype(jnp.float32)
    group_power = lax.dot_general(
        member_hot, jnp.square(values), (((0,), (0,)), ((), ())), precision=lax.Precision.HIGHEST
    )
    counts = jnp.sum(member_hot, axis=0)
    inverse_noise = (counts + 1.0)[:, None] / (group_power + 1.0)
    whitened = (values * inverse_noise[member]).astype(jnp.bfloat16)
    panel_block = lax.all_gather(references, "cls", axis=0, tiled=True)
    held = panel_block.shape[0]
    flat_panels = panel_block.reshape(held * bins_all, voxels)
    correlation = lax.dot_general(
        whitened, flat_panels, (((1,), (1,)), ((), ())), preferred_element_type=jnp.float32
    )
    energy = lax.dot_general(
        inverse_noise,
        jnp.square(flat_panels.astype(jnp.float32)),
        (((1,), (1,)), ((), ())),
        precision=lax.Precision.HIGHEST,
    )
    combined = (correlation - 0.5 * energy[member]) * (1.0 / math.sqrt(voxels))
    orient_hot = (orient[:, None] == jnp.arange(bins_all, dtype=jnp.int32)[None, :]).astype(
        jnp.float32
    )
    scores = jnp.sum(
        combined.reshape(slot_count, classes, bins_all) * orient_hot[:, None, :], axis=2
    )
    weights = (jax.nn.softmax(scores, axis=1) * occupied[:, None].astype(jnp.float32)).astype(
        jnp.bfloat16
    )
    coefficient = (weights[:, :, None] * orient_hot[:, None, :].astype(jnp.bfloat16)).reshape(
        slot_count, classes * bins_all
    )
    weight_sum = jnp.sum(coefficient.astype(jnp.float32), axis=0)
    totals = lax.psum(weight_sum, ("cls", "dom"))
    accumulated = lax.dot_general(
        coefficient, whitened, (((0,), (0,)), ((), ())), preferred_element_type=jnp.float32
    )
    stacked = accumulated.reshape(classes, bins_all, voxels)
    slab_part = lax.psum_scatter(stacked, "dom", scatter_dimension=2, tiled=True)
    own_slab = lax.psum_scatter(slab_part, "cls", scatter_dimension=0, tiled=True)
    own_totals = lax.dynamic_slice_in_dim(
        totals.reshape(classes, bins_all), lax.axis_index("cls") * block_classes, block_classes, 0
    )
    return own_slab / (own_totals[:, :, None] + 1.0)


def solution(mesh):
    in_specs = (
        P(("cls", "dom"), None),
        P("cls", None, None),
        P(("cls", "dom")),
        P(("cls", "dom"), None),
        P(("cls", "dom")),
    )
    out_specs = P("cls", None, "dom")
    return jax.shard_map(shards, mesh=mesh, in_specs=in_specs, out_specs=out_specs, check_vma=False)
```

profile of v0, /device:TPU:1, one launch (start us, length us, event | category | flops | bytes accessed | tf_op | source)
XLA Modules:
  0.0 536.5 jit_solution(9709265180745902310)
XLA Ops:
  6.5 0.9 fusion.18
  7.5 0.8 select_reduce_fusion.1
  8.3 0.7 add_convert_fusion
  9.0 0.1 select_reduce_fusion
  9.1 0.7 convert_element_type.145
  9.8 12.6 %all-to-all-start.1 = ((bf16[32,1,2]{2,1,0:T(2,128)(2,1)}), bf16[32,1,2]{2,1,0:T(2,128)(2,1)S(1)}, u32[]{:S(2)}, u32[]{:S(2)}) async-start(bf16[32,1,2]{2,1,0:T(2,128)(2,1)} %convert_element_type.145), calls=%async_computation.1 | async-start | bytes 32768 | tf_op jit(solution)/shard_map/all_to_all | solution.py:41
  22.4 3.3 convolution_convert_fusion
  25.7 7.7 %reshape.249 = bf16[32,2,32768]{2,1,0:T(2,128)(2,1)} reshape(bf16[64,32768]{1,0:T(8,128)(2,1)} %convolution_convert_fusion) | data formatting | bytes 8388608 | tf_op jit(solution)/shard_map/reshape | solution.py:35
  33.4 9.9 %all-to-all-start = ((bf16[32,2,32768]{2,1,0:T(2,128)(2,1)}), bf16[32,2,32768]{2,1,0:T(2,128)(2,1)}, u32[]{:S(2)}, u32[]{:S(2)}) async-start(bf16[32,2,32768]{2,1,0:T(2,128)(2,1)} %reshape.249), calls=%async_computation | async-start | bytes 8388608 | tf_op jit(solution)/shard_map/all_to_all | solution.py:34
  43.3 0.7 all-gather.2.cloned.1.call-update
  44.1 0.1 convert_add_fusion
  44.1 0.1 sub.35
  44.2 0.1 sub.36
  44.4 0.1 convert_reduce_fusion.1
  44.5 94.9 %all-to-all-done = bf16[32,2,32768]{2,1,0:T(2,128)(2,1)} async-done(((bf16[32,2,32768]{2,1,0:T(2,128)(2,1)}), bf16[32,2,32768]{2,1,0:T(2,128)(2,1)}, u32[]{:S(2)}, u32[]{:S(2)}) %all-to-all-start) | async-done | bytes 4194336 | tf_op jit(solution)/shard_map/all_to_all | solution.py:34
  139.4 6.0 %convert_multiply_fusion.1 = f32[8,8,32768]{2,1,0:T(8,128)} fusion(bf16[8,8,32768]{2,1,0:T(8,128)(2,1)} %bitcast.32), kind=kLoop, calls=%fused_computation.9 | loop fusion | flops 4194304 | bytes 12582912 | tf_op jit(solution)/shard_map/square | solution.py:59
  145.4 11.0 %square.10 = f32[64,32768]{1,0:T(8,128)} reshape(f32[32,2,32768]{2,1,0:T(2,128)} %bitcast.34) | data formatting | bytes 16777216 | tf_op jit(solution)/shard_map/square | solution.py:59
  156.4 5.2 fusion
  161.6 6.0 %gather_fusion = f32[64,32768]{1,0:T(8,128)} fusion(f32[8,32768]{1,0:T(8,128)S(1)} %fusion, s32[1024]{0:T(1024)S(1)} %pad_clamp_fusion), kind=kCustom, calls=%fused_computation | custom fusion | bytes 16777472 | tf_op jit(solution)/shard_map/gather | solution.py:63
  167.6 10.6 %gather.9 = f32[32,2,32768]{2,1,0:T(2,128)} reshape(f32[64,32768]{1,0:T(8,128)} %gather_fusion) | data formatting | bytes 16777216 | tf_op jit(solution)/shard_map/gather | solution.py:63
  178.2 8.1 %fusion.4 = bf16[32,2,32768]{2,1,0:T(2,128)(2,1)} fusion(f32[32,2,32768]{2,1,0:T(2,128)} %gather.9, bf16[32,2,32768]{2,1,0:T(2,128)(2,1)} %all-to-all-done), kind=kLoop, calls=%fused_computation.10 | loop fusion | flops 6291456 | bytes 16777216 | tf_op jit(solution)/shard_map/convert_element_type | solution.py:63
  186.3 7.2 %convert_element_type.138 = bf16[64,32768]{1,0:T(8,128)(2,1)} reshape(bf16[32,2,32768]{2,1,0:T(2,128)(2,1)} %fusion.4) | data formatting | bytes 8388608 | tf_op jit(solution)/shard_map/convert_element_type | solution.py:63
  193.6 7.2 %reshape.270 = bf16[64,32768,1]{1,0,2:T(8,128)(2,1)} reshape(bf16[32,2,32768]{2,1,0:T(2,128)(2,1)} %fusion.4) | data formatting | bytes 8388608 | tf_op jit(solution)/shard_map/convert_element_type | solution.py:63
  200.8 15.4 %fusion.1 = f32[8,128]{1,0:T(8,128)S(1)} fusion(f32[8,32768]{1,0:T(8,128)S(1)} %fusion, bf16[16,8,32768]{2,1,0:T(8,128)(2,1)} %all-gather.2.cloned.1.call-done), kind=kOutput, calls=%fused_computation.5 | convolution fusion | flops 411041792 | bytes 9441280 | tf_op jit(solution)/shard_map/dot_general | solution.py:70
  216.1 0.6 gather_fusion.1
  216.8 7.7 %fusion.11 = f32[64,128]{1,0:T(8,128)S(1)} fusion(bf16[64,32768]{1,0:T(8,128)(2,1)} %convert_element_type.138, bf16[16,8,32768]{2,1,0:T(8,128)(2,1)} %all-gather.2.cloned.1.call-done, f32[64,128]{1,0:T(8,128)S(1)} %gather_fusion.1), kind=kOutput, calls=%fused_computation.15 | convolution fusion | flops 536895488 | bytes 12648448 | tf_op jit(solution)/shard_map/dot_general | solution.py:67
  224.4 0.1 copy.11
  224.6 10.2 %fusion.15 = f32[16,8,32768]{2,1,0:T(8,128)} fusion(bf16[64,32768,1]{1,0,2:T(8,128)(2,1)} %reshape.270, bf16[64,8]{0,1:T(8,128)(2,1)S(1)} %get-tuple-element.10, bf16[64,16]{0,1:T(8,128)(2,1)S(1)} %multiply_convert_fusion), kind=kOutput, calls=%fused_computation.20 | convolution fusion | flops 536879104 | bytes 20974592 | tf_op jit(solution)/shard_map/dot_general | solution.py:91
  234.9 214.7 %reduce-scatter.3.cloned.1.call-done = f32[16,8,1024]{2,1,0:T(8,128)} async-done(((f32[16,8,32768]{2,1,0:T(8,128)}), f32[16,8,1024]{2,1,0:T(8,128)}) %reduce-scatter.3.cloned.1.call-update) | async-done | bytes 524304 | tf_op jit(solution)/shard_map/reduce_scatter | solution.py:95
  449.6 0.1 convert_reduce_fusion
  449.7 78.7 %psum.7 = f32[16,8]{1,0:T(8,128)S(1)} all-reduce(f32[16,8]{1,0:T(8,128)S(1)} %convert_reduce_fusion), channel_id=1, replica_groups=mesh['cls'=8,'dom'=32] {'cls','dom'}, use_global_device_ids=true, to_apply=%region_10.11 | all-reduce | flops 128 | bytes 1024 | tf_op jit(solution)/shard_map/psum | solution.py:90
  528.5 1.5 broadcast_divide_fusion
  (24 shorter events, 0.4 us)
Async XLA Ops:
  6.5 15.9 %copy-start = (bf16[32,32768]{1,0:T(8,128)(2,1)S(1)}, bf16[32,32768]{1,0:T(8,128)(2,1)}, u32[]{:S(2)}) copy-start(bf16[32,32768]{1,0:T(8,128)(2,1)} %param.5) | copy-start | bytes 6291460
  9.8 23.6 %all-to-all-start.1 = ((bf16[32,1,2]{2,1,0:T(2,128)(2,1)}), bf16[32,1,2]{2,1,0:T(2,128)(2,1)S(1)}, u32[]{:S(2)}, u32[]{:S(2)}) async-start(bf16[32,1,2]{2,1,0:T(2,128)(2,1)} %convert_element_type.145), calls=%async_computation.1 | async-start | bytes 32768 | tf_op jit(solution)/shard_map/all_to_all | solution.py:41
  33.4 106.0 %all-to-all-start = ((bf16[32,2,32768]{2,1,0:T(2,128)(2,1)}), bf16[32,2,32768]{2,1,0:T(2,128)(2,1)}, u32[]{:S(2)}, u32[]{:S(2)}) async-start(bf16[32,2,32768]{2,1,0:T(2,128)(2,1)} %reshape.249), calls=%async_computation | async-start | bytes 8388608 | tf_op jit(solution)/shard_map/all_to_all | solution.py:34
  43.3 157.5 %all-gather.2.cloned.1.call-start = ((), (), s32[]{:S(2)}) async-start(), calls=%async_computation.4 | async-start | bytes 9437184 | tf_op jit(solution)/shard_map/all_gather | solution.py:64
  44.0 405.6 %reduce-scatter.3.cloned.1.call-start = ((), (), s32[]{:S(2)}) async-start(), calls=%async_computation.5 | async-start | bytes 17301504 | tf_op jit(solution)/shard_map/reduce_scatter | solution.py:95
  234.8 295.2 %copy-start.1 = (bf16[32,32768]{1,0:T(8,128)(2,1)S(1)}, bf16[32,32768]{1,0:T(8,128)(2,1)}, u32[]{:S(2)}) copy-start(bf16[32,32768]{1,0:T(8,128)(2,1)} %param.5) | copy-start | bytes 6291460
  234.9 293.6 %reduce-scatter.5.cloned.1.call-start = ((), (), s32[]{:S(2)}) async-start(), calls=%async_computation.6 | async-start | bytes 589824 | tf_op jit(solution)/shard_map/reduce_scatter | solution.py:96
Sparse Core Ops, SparseCore 0:
  45.9 129.8 all-gather.1
  235.0 214.5 reduce-scatter.2
  452.3 37.6 reduce-scatter.4
where the time goes:
time: 538 us; the launch traced here: 537 us
  waiting for transfers between devices  310 us (58%)
  blocking collectives  78.7 us (15%)
  local copies, waits for them, and re-layouts  51.3 us (10%)
  matrix products  41.7 us (8%)
  starting transfers between devices  22.6 us (4%)
  other arithmetic  18.6 us (3%)
  between operations  13.2 us (2%)
    reduce_scatter x1, waiting for transfers between devices, shards(): lax.psum_scatter(stacked, 'dom', scatter_dimension=2, tiled=True)  215 us
    all_to_all x1, waiting for transfers between devices, shards(): lax.all_to_all(outgoing.reshape(sources, capacity, voxels), 'dom', split_...  94.9 us
    psum x1, blocking collectives, shards(): totals = lax.psum(weight_sum, ('cls', 'dom'))  78.7 us
    gather x2, local copies, waits for them, and re-layouts, shards(): whitened = (values * inverse_noise[member]).astype(jnp.bfloat16)  16.6 us
    dot_general x1, matrix products, shards(): lax.dot_general(inverse_noise, jnp.square(flat_panels.astype(jnp.float32)...  15.4 us
    convert_element_type x2, local copies, waits for them, and re-layouts, shards(): whitened = (values * inverse_noise[member]).astype(jnp.bfloat16)  14.5 us
    all_to_all x1, starting transfers between devices, shards(): lax.all_to_all(outgoing_codes.reshape(sources, capacity), 'dom', split_ax...  12.6 us
    square x1, local copies, waits for them, and re-layouts, shards(): jnp.square(values)  11 us
  transfers between devices with their start and end apart: 5, of which 2 were waited for; matrix products, arithmetic and copies ran while one was open for 14% of the time, Pallas kernels for 0%

commit v1 on v0

v1 whole, which is shorter than its diff:
```python
import math

import jax
import jax.numpy as jnp
from jax import lax
from jax.sharding import PartitionSpec as P


def shards(particles, references, orient_bins, destinations, group_slots):
    sources = lax.axis_size("dom")
    rows, voxels = particles.shape
    block_classes, bins_all, _ = references.shape
    classes = block_classes * lax.axis_size("cls")
    groups = 8 * sources
    slab = voxels // sources
    members = rows * sources

    codes = (destinations[:, 0] * 8 + group_slots) * bins_all + orient_bins
    codes = lax.all_gather(codes, "dom", axis=0, tiled=True)
    group = codes // bins_all
    orient = codes % bins_all
    own = lax.dynamic_slice_in_dim(references, lax.axis_index("dom") * slab, slab, 2)
    panels = lax.all_gather(own, "cls", axis=0, tiled=True).reshape(classes * bins_all, slab)

    values = lax.all_to_all(
        particles.reshape(rows, sources, slab), "dom", split_axis=1, concat_axis=0, tiled=True
    ).reshape(members, slab)

    hot = (group[:, None] == jnp.arange(groups, dtype=jnp.int32)[None, :]).astype(jnp.float32)
    wide = values.astype(jnp.float32)
    power = lax.dot_general(
        hot, jnp.square(wide), (((0,), (0,)), ((), ())), precision=lax.Precision.HIGHEST
    )
    counts = jnp.sum(hot, axis=0)
    inverse_noise = (counts + 1.0)[:, None] / (power + 1.0)
    spread = jnp.dot(hot, inverse_noise, precision=lax.Precision.HIGHEST)
    whitened = (wide * spread).astype(jnp.bfloat16)
    correlation = lax.dot_general(
        whitened, panels, (((1,), (1,)), ((), ())), preferred_element_type=jnp.float32
    )
    energy = lax.dot_general(
        inverse_noise,
        jnp.square(panels.astype(jnp.float32)),
        (((1,), (1,)), ((), ())),
        precision=lax.Precision.HIGHEST,
    )
    combined = correlation - 0.5 * jnp.dot(hot, energy, precision=lax.Precision.HIGHEST)
    orient_hot = orient[:, None] == jnp.arange(bins_all, dtype=jnp.int32)[None, :]
    partial = jnp.sum(
        jnp.where(orient_hot[:, None, :], combined.reshape(members, classes, bins_all), 0.0), axis=2
    )
    scores = lax.psum(partial, "dom") * (1.0 / math.sqrt(voxels))
    weights = jax.nn.softmax(scores, axis=1).astype(jnp.bfloat16)
    coefficient = (weights[:, :, None] * orient_hot[:, None, :].astype(jnp.bfloat16)).reshape(
        members, classes * bins_all
    )
    weight_sum = jnp.sum(coefficient.astype(jnp.float32), axis=0)
    accumulated = lax.dot_general(
        coefficient, whitened, (((0,), (0,)), ((), ())), preferred_element_type=jnp.float32
    )
    own_slab = lax.psum_scatter(
        accumulated.reshape(classes, bins_all, slab), "cls", scatter_dimension=0, tiled=True
    )
    totals = lax.psum(weight_sum, "cls").reshape(classes, bins_all)
    own_totals = lax.dynamic_slice_in_dim(
        totals, lax.axis_index("cls") * block_classes, block_classes, 0
    )
    return own_slab / (own_totals[:, :, None] + 1.0)


def solution(mesh):
    in_specs = (
        P(("cls", "dom"), None),
        P("cls", None, None),
        P(("cls", "dom")),
        P(("cls", "dom"), None),
        P(("cls", "dom")),
    )
    out_specs = P("cls", None, "dom")
    return jax.shard_map(shards, mesh=mesh, in_specs=in_specs, out_specs=out_specs, check_vma=False)
```

time: 538 us -> 399 us (0.74)
  waiting for transfers between devices: 310 us -> 255 us
  local copies, waits for them, and re-layouts: 51.3 us -> 3.89 us
  matrix products: 41.7 us -> 10.6 us
  blocking collectives: 78.7 us -> 92.4 us
  other arithmetic: 18.6 us -> 5.22 us
  starting transfers between devices: 22.6 us -> 12.8 us
    psum x0 -> x1, waiting for transfers between devices: none -> 238 us  [shards(): scores = lax.psum(partial, 'dom') * (1.0 / math.sqrt(voxels))]
    reduce_scatter x2 -> x1, waiting for transfers between devices: 215 us -> 17 us  [shards(): lax.psum_scatter(accumulated.reshape(classes, bins_all, slab), 'cls', sca...]
    all_to_all x2 -> x1, waiting for transfers between devices: 94.9 us -> 0.01 us  [shards(): lax.all_to_all(particles.reshape(rows, sources, slab), 'dom', split_axis=...]
    psum x1, blocking collectives: 78.7 us -> 15.2 us  [shards(): totals = lax.psum(weight_sum, 'cls').reshape(classes, bins_all)]
    unnamed x0 -> x1, blocking collectives: none -> 54.8 us
    dot_general x4 -> x5, matrix products: 31.5 us -> 7.77 us  [the longest x1 2.43 us: shards(): lax.dot_general(hot, jnp.square(wide), (((0,), (0,)), ((), ())), precisio...]
    all_gather x0 -> x1, blocking collectives: none -> 22.4 us  [shards(): lax.all_gather(own, 'cls', axis=0, tiled=True)]
    gather x3 -> x0, local copies, waits for them, and re-layouts: 17.2 us -> none  [the longest x2 16.6 us: shards(): whitened = (values * inverse_noise[member]).astype(jnp.bfloat16)]
  transfers between devices with their start and end apart: 5 -> 3, of which waited for: 2 -> 2; matrix products, arithmetic and copies ran while one was open for 14% -> 0% of each run, Pallas kernels for 0% -> 0%
where the time goes in v1:
time: 399 us; the launch traced here: 395 us
  waiting for transfers between devices  255 us (64%)
  blocking collectives  92.4 us (23%)
  between operations  14.2 us (4%)
  starting transfers between devices  12.8 us (3%)
  matrix products  10.6 us (3%)
  other arithmetic  5.22 us (1%)
    psum x1, waiting for transfers between devices, shards(): scores = lax.psum(partial, 'dom') * (1.0 / math.sqrt(voxels))  238 us
    unnamed x1, blocking collectives  54.8 us
    all_gather x1, blocking collectives, shards(): lax.all_gather(own, 'cls', axis=0, tiled=True)  22.4 us
    reduce_scatter x1, waiting for transfers between devices, shards(): lax.psum_scatter(accumulated.reshape(classes, bins_all, slab), 'cls', sca...  17 us
    psum x1, blocking collectives, shards(): totals = lax.psum(weight_sum, 'cls').reshape(classes, bins_all)  15.2 us
    all_to_all x1, starting transfers between devices, shards(): lax.all_to_all(particles.reshape(rows, sources, slab), 'dom', split_axis=...  12.7 us
  transfers between devices with their start and end apart: 3, of which 2 were waited for; matrix products, arithmetic and copies ran while one was open for 0% of the time, Pallas kernels for 0%

profile of v1, /device:TPU:1, one launch (start us, length us, event | category | flops | bytes accessed | tf_op | source)
XLA Modules:
  0.0 394.5 jit_solution(2403567844912491047)
XLA Ops:
  6.5 0.0 copy-start
  6.5 3.3 copy.11
  9.8 12.7 %all-to-all-start = ((bf16[32,32,1024]{2,0,1:T(8,128)(2,1)}), bf16[32,32,1024]{2,0,1:T(8,128)(2,1)S(1)}, u32[]{:S(2)}, u32[]{:S(2)}) async-start(bf16[32,32,1024]{2,0,1:T(8,128)(2,1)} %bitcast.52), calls=%async_computation | async-start | bytes 4194304 | tf_op jit(solution)/shard_map/all_to_all | solution.py:25
  22.6 0.0 all-reduce.3.cloned.1.call-start
  22.6 0.0 copy-done.5
  22.6 0.6 dynamic-slice
  23.9 0.0 copy-done.2
  23.9 0.0 copy-done.3
  23.9 0.0 copy-done.4
  23.9 0.1 fusion.24
  24.0 54.8 %all-reduce = s32[1024]{0:T(1024)S(1)} all-reduce(s32[1024]{0:T(1024)S(1)} %fusion.24), channel_id=1, replica_groups=mesh['cls'=8,'dom'=32] {'dom'}, use_global_device_ids=true, to_apply=%add | all-reduce | flops 1024 | bytes 8192
  78.9 22.4 %all_gather.7 = bf16[16,8,1024]{2,1,0:T(8,128)(2,1)S(1)} all-gather(bf16[2,8,1024]{2,1,0:T(8,128)(2,1)S(1)} %constant_dynamic-slice_fusion), channel_id=1, replica_groups=mesh['cls'=8,'dom'=32] {'cls'}, dimensions={0}, use_global_device_ids=true | all-gather | bytes 294912 | tf_op jit(solution)/shard_map/all_gather | solution.py:23
  101.3 0.2 convert_reduce_fusion
  101.5 0.0 all-to-all-done
  101.6 0.6 bitcast_multiply_fusion.1
  102.1 2.4 fusion.3
  104.6 2.0 fusion
  106.6 1.0 fusion.8
  107.6 0.8 fusion.15
  108.4 1.5 fusion.7
  110.0 0.0 all-reduce.3.cloned.1.call-update
  110.0 0.0 reduce-scatter.2.cloned.1.call-start
  110.0 238.3 %all-reduce.3.cloned.1.call-done = f32[1024,16]{0,1:T(8,128)} async-done(((f32[1024,16]{0,1:T(8,128)}), f32[1024,16]{0,1:T(8,128)}) %all-reduce.3.cloned.1.call-update) | async-done | bytes 65552 | tf_op jit(solution)/shard_map/psum | solution.py:52
  348.3 0.9 multiply_reduce_fusion
  349.2 0.9 fusion.19
  350.0 0.9 divide_convert_fusion
  350.9 2.8 fusion.1
  353.8 0.0 reduce-scatter.2.cloned.1.call-update
  353.8 0.1 convert_reduce_fusion.1
  353.9 15.2 %psum.15 = f32[16,8]{1,0:T(8,128)S(1)} all-reduce(f32[16,8]{1,0:T(8,128)S(1)} %convert_reduce_fusion.1), channel_id=1, replica_groups=mesh['cls'=8,'dom'=32] {'cls'}, use_global_device_ids=true, to_apply=%region_7.8 | all-reduce | flops 128 | bytes 1024 | tf_op jit(solution)/shard_map/psum | solution.py:64
  369.1 17.0 %reduce-scatter.2.cloned.1.call-done = f32[2,8,1024]{2,1,0:T(8,128)} async-done(((f32[16,8,1024]{2,1,0:T(8,128)}), f32[2,8,1024]{2,1,0:T(8,128)}) %reduce-scatter.2.cloned.1.call-update) | async-done | bytes 65552 | tf_op jit(solution)/shard_map/reduce_scatter | solution.py:61
  386.1 1.5 broadcast_divide_fusion
  (13 shorter events, 0.1 us)
Async XLA Ops:
  6.5 72.3 %copy-start = (bf16[2,8,32768]{2,1,0:T(8,128)(2,1)S(1)}, bf16[2,8,32768]{2,1,0:T(8,128)(2,1)}, u32[]{:S(2)}) copy-start(bf16[2,8,32768]{2,1,0:T(8,128)(2,1)} %param.6) | copy-start | bytes 3145732
  9.8 12.8 %copy-start.5 = (u32[256]{0:T(256)S(1)}, u32[256]{0:T(256)}, u32[]{:S(2)}) copy-start(u32[256]{0:T(256)} %constant.67) | copy-start | bytes 3076
  9.8 14.1 %copy-start.2 = (s32[32]{0:T(128)S(1)}, s32[32]{0:T(128)}, u32[]{:S(2)}) copy-start(s32[32]{0:T(128)} %param.7) | copy-start | bytes 388
  9.8 14.1 %copy-start.3 = (s32[32]{0:T(128)S(1)}, s32[32]{0:T(128)}, u32[]{:S(2)}) copy-start(s32[32]{0:T(128)} %param.9) | copy-start | bytes 388
  9.8 14.1 %copy-start.4 = (s32[32,1]{0,1:T(1,128)S(1)}, s32[32,1]{0,1:T(1,128)}, u32[]{:S(2)}) copy-start(s32[32,1]{0,1:T(1,128)} %param.8) | copy-start | bytes 388
  9.8 91.7 %all-to-all-start = ((bf16[32,32,1024]{2,0,1:T(8,128)(2,1)}), bf16[32,32,1024]{2,0,1:T(8,128)(2,1)S(1)}, u32[]{:S(2)}, u32[]{:S(2)}) async-start(bf16[32,32,1024]{2,0,1:T(8,128)(2,1)} %bitcast.52), calls=%async_computation | async-start | bytes 4194304 | tf_op jit(solution)/shard_map/all_to_all | solution.py:25
  22.6 325.8 %all-reduce.3.cloned.1.call-start = ((), (), s32[]{:S(2)}) async-start(), calls=%async_computation.2 | async-start | bytes 131072 | tf_op jit(solution)/shard_map/psum | solution.py:52
  106.6 1.8 copy-start.1
  110.0 276.1 %reduce-scatter.2.cloned.1.call-start = ((), (), s32[]{:S(2)}) async-start(), calls=%async_computation.3 | async-start | bytes 589824 | tf_op jit(solution)/shard_map/reduce_scatter | solution.py:61
Sparse Core Ops, SparseCore 0:
  110.1 238.1 all-reduce.2
  353.9 32.1 reduce-scatter.1

commit v2 on v1

v2 whole, which is shorter than its diff:
```python
import functools
import math

import jax
import jax.numpy as jnp
from jax import lax
from jax.experimental import pallas as pl
from jax.experimental.pallas import tpu as pltpu
from jax.sharding import PartitionSpec as P

MESH = pl.DeviceIdType.MESH
F32 = jnp.float32
BF16 = jnp.bfloat16

ROWS = 32
DOM = 32
CLS = 8
BINS = 8
CLASSES = 16
GROUPS = 256
MEMBERS = ROWS * DOM
SLAB = 1024
CHUNKS = 4
WIDE = SLAB // CHUNKS
PANELS = CLASSES * BINS
OWN = PANELS // CLS
Z = 8

NT = (((1,), (1,)), ((), ()))


def dot(a, b):
    return jnp.dot(a, b, preferred_element_type=F32)


def dot_nt(a, b):
    return lax.dot_general(a, b, NT, preferred_element_type=F32)


def split(value, pieces):
    out = []
    for _ in range(pieces):
        piece = value.astype(BF16)
        out.append(piece)
        value = value - piece.astype(F32)
    return out


def dom_peer(i, dom):
    core, z, x = dom % 2, (dom // 2) % Z, dom // (2 * Z)
    j = i // 4
    step = 4 + (1 - 2 * (j % 2)) * ((j + 1) // 2)
    core = (core + 1 - i % 2) % 2
    x = (x + 1 - (i // 2) % 2) % 2
    z = (z + step) % Z
    return (x * Z + z) * 2 + core


def kernel(
    particles,
    references,
    codes,
    out,
    x_ref,
    r_ref,
    c_ref,
    hot_t,
    hot,
    score_sum,
    energy_sum,
    piece_out,
    piece_in,
    piece_all,
    scores_ref,
    acc_out,
    acc_in,
    tot_out,
    tot_in,
    x_recv,
    misc_recv,
    send,
    local,
):
    cls = lax.axis_index("cls")
    dom = lax.axis_index("dom")

    barrier = pltpu.get_barrier_semaphore()

    def greet_dom(i, carry):
        pl.semaphore_signal(barrier, inc=1, device_id=(cls, dom_peer(i, dom)), device_id_type=MESH)
        return carry

    def greet_cls(i, carry):
        pl.semaphore_signal(barrier, inc=1, device_id=((cls + i) % CLS, dom), device_id_type=MESH)
        return carry

    lax.fori_loop(0, DOM - 1, greet_dom, 0)
    lax.fori_loop(1, CLS, greet_cls, 0)
    pl.semaphore_wait(barrier, DOM - 1 + CLS - 1)

    def send_to(src, dst, sem_out, sem_in, device):
        pltpu.make_async_remote_copy(
            src_ref=src,
            dst_ref=dst,
            send_sem=sem_out,
            recv_sem=sem_in,
            device_id=device,
            device_id_type=MESH,
        ).start()

    def taken(ref, sem):
        pltpu.make_async_copy(ref, ref, sem).wait()

    def send_codes(i, carry):
        send_to(codes, c_ref.at[dom], send.at[0], misc_recv.at[0], (cls, dom_peer(i, dom)))
        return carry

    def send_panels(i, carry):
        send_to(references, r_ref.at[cls], send.at[1], misc_recv.at[1], ((cls + i) % CLS, dom))
        return carry

    lax.fori_loop(0, DOM - 1, send_codes, 0)
    lax.fori_loop(1, CLS, send_panels, 0)

    def send_chunk(k, carry):
        chunk, i = k // (DOM - 1), k % (DOM - 1)
        peer = dom_peer(i, dom)
        start = pl.multiple_of(peer * SLAB + chunk * WIDE, WIDE)
        send_to(
            particles.at[:, pl.ds(start, WIDE)],
            x_ref.at[chunk, dom],
            send.at[2],
            x_recv.at[chunk],
            (cls, peer),
        )
        return carry

    lax.fori_loop(0, CHUNKS * (DOM - 1), send_chunk, 0)

    own_copies = []
    for chunk in range(CHUNKS):
        start = pl.multiple_of(dom * SLAB + chunk * WIDE, WIDE)
        own_copies.append(
            pltpu.make_async_copy(
                particles.at[:, pl.ds(start, WIDE)], x_ref.at[chunk, dom], local.at[chunk]
            )
        )
    for copy in own_copies:
        copy.start()
    c_ref[dom] = codes[...]
    r_ref[cls] = references[...]

    taken(c_ref.at[pl.ds(0, DOM - 1)], misc_recv.at[0])
    code = jnp.sum(c_ref[...].reshape(8, 4, 128), axis=1)
    code_row = jnp.concatenate([code[t : t + 1] for t in range(8)], axis=1)
    group_row = code_row // BINS
    orient_row = code_row % BINS
    members = jnp.broadcast_to(group_row, (GROUPS, MEMBERS))
    hot_f32 = (lax.broadcasted_iota(jnp.int32, (GROUPS, MEMBERS), 0) == members).astype(F32)
    hot_t[...] = hot_f32.astype(BF16)
    counts = jnp.sum(hot_f32, axis=1, keepdims=True)
    group_col = jnp.transpose(jnp.broadcast_to(group_row.astype(F32), (128, MEMBERS)))
    lanes = lax.broadcasted_iota(jnp.int32, (MEMBERS, 128), 1).astype(F32)
    for half in range(GROUPS // 128):
        hot[:, 128 * half : 128 * half + 128] = (
            (group_col == lanes + float(128 * half)).astype(F32).astype(BF16)
        )
    score_sum[...] = jnp.zeros_like(score_sum)
    energy_sum[...] = jnp.zeros_like(energy_sum)

    taken(r_ref.at[pl.ds(0, CLS - 1)], misc_recv.at[1])
    for copy in own_copies:
        copy.wait()

    def whiten(chunk, carry):
        taken(x_ref.at[chunk, pl.ds(0, DOM - 1)], x_recv.at[chunk])
        values = x_ref[chunk].reshape(MEMBERS, WIDE).astype(F32)
        high, low = split(values * values, 2)
        power = dot(hot_t[...], high) + dot(hot_t[...], low)
        inverse = (counts + 1.0) / (power + 1.0)
        parts = split(inverse, 3)
        spread = dot(hot[...], parts[0]) + dot(hot[...], parts[1])
        whitened = (values * spread).astype(BF16)
        x_ref[chunk] = whitened.reshape(DOM, ROWS, WIDE)
        panels = r_ref[:, :, pl.ds(pl.multiple_of(chunk * WIDE, WIDE), WIDE)].reshape(PANELS, WIDE)
        score_sum[...] += dot_nt(panels, whitened)
        wide = panels.astype(F32)
        square = split(wide * wide, 2)
        energy = jnp.zeros((PANELS, GROUPS), F32)
        for piece in square:
            for part in parts:
                energy += dot_nt(piece, part)
        energy_sum[...] += energy
        return carry

    lax.fori_loop(0, CHUNKS, whiten, 0)

    spread_energy = jnp.zeros((PANELS, MEMBERS), F32)
    for part in split(energy_sum[...], 3):
        spread_energy += dot(part, hot_t[...])
    combined = (score_sum[...] - 0.5 * spread_energy).reshape(CLASSES, BINS, MEMBERS)
    bin_index = lax.broadcasted_iota(jnp.int32, (BINS, MEMBERS), 0)
    in_bin = bin_index == jnp.broadcast_to(orient_row, (BINS, MEMBERS))
    partial = jnp.sum(jnp.where(in_bin[None], combined, 0.0), axis=1)
    for q in range(4):
        for t in range(8):
            piece_out[q * 8 + t] = partial[4 * q : 4 * q + 4, 128 * t : 128 * t + 128]

    def send_piece(i, carry):
        peer = dom_peer(i, dom)
        send_to(piece_out.at[peer], piece_in.at[dom], send.at[3], misc_recv.at[2], (cls, peer))
        return carry

    lax.fori_loop(0, DOM - 1, send_piece, 0)
    piece_in[dom] = piece_out[dom]
    taken(piece_in.at[pl.ds(0, DOM - 1)], misc_recv.at[2])
    piece_all[dom] = jnp.sum(piece_in[...], axis=0)

    def send_sum(i, carry):
        peer = dom_peer(i, dom)
        send_to(piece_all.at[dom], piece_all.at[dom], send.at[4], misc_recv.at[3], (cls, peer))
        return carry

    lax.fori_loop(0, DOM - 1, send_sum, 0)
    taken(piece_all.at[pl.ds(0, DOM - 1)], misc_recv.at[3])
    for q in range(4):
        for t in range(8):
            scores_ref[4 * q : 4 * q + 4, 128 * t : 128 * t + 128] = piece_all[q * 8 + t]

    scores = scores_ref[...] * (1.0 / math.sqrt(DOM * SLAB))
    power = jnp.exp(scores - jnp.max(scores, axis=0, keepdims=True))
    weights = (power / jnp.sum(power, axis=0, keepdims=True)).astype(BF16).astype(F32)
    coefficient_f32 = jnp.where(in_bin[None], weights[:, None, :], 0.0).reshape(PANELS, MEMBERS)
    coefficient = coefficient_f32.astype(BF16)
    totals = jnp.sum(coefficient_f32, axis=1, keepdims=True)
    tot_out[...] = jnp.broadcast_to(totals, (PANELS, 128)).reshape(CLS, OWN, 128)

    def send_total(i, carry):
        peer = (cls + i) % CLS
        send_to(tot_out.at[peer], tot_in.at[cls], send.at[5], misc_recv.at[4], (peer, dom))
        return carry

    lax.fori_loop(1, CLS, send_total, 0)
    tot_in[cls] = tot_out[cls]

    for chunk in range(CHUNKS):
        acc_out[:, :, chunk * WIDE : (chunk + 1) * WIDE] = (
            dot(coefficient, x_ref[chunk].reshape(MEMBERS, WIDE))
            .astype(acc_out.dtype)
            .reshape(CLS, OWN, WIDE)
        )

    def send_acc(i, carry):
        peer = (cls + i) % CLS
        send_to(acc_out.at[peer], acc_in.at[cls], send.at[6], misc_recv.at[5], (peer, dom))
        return carry

    lax.fori_loop(1, CLS, send_acc, 0)
    acc_in[cls] = acc_out[cls]
    taken(tot_in.at[pl.ds(0, CLS - 1)], misc_recv.at[4])
    total = jnp.sum(tot_in[...], axis=0)[:, 0:1]
    taken(acc_in.at[pl.ds(0, CLS - 1)], misc_recv.at[5])
    out[...] = jnp.sum(acc_in[...].astype(F32), axis=0) / (total + 1.0)

    taken(c_ref.at[pl.ds(0, DOM - 1)], send.at[0])
    taken(r_ref.at[pl.ds(0, CLS - 1)], send.at[1])
    taken(x_ref.at[:, pl.ds(0, DOM - 1)], send.at[2])
    taken(piece_in.at[pl.ds(0, DOM - 1)], send.at[3])
    taken(piece_all.at[pl.ds(0, DOM - 1)], send.at[4])
    taken(tot_in.at[pl.ds(0, CLS - 1)], send.at[5])
    taken(acc_in.at[pl.ds(0, CLS - 1)], send.at[6])


def shards(particles, references, orient_bins, destinations, group_slots):
    dom = lax.axis_index("dom")
    code = (destinations[:, 0] * 8 + group_slots) * BINS + orient_bins
    lane = jnp.arange(128, dtype=jnp.int32)
    codes = jnp.where(lane // ROWS == dom % 4, jnp.tile(code, 4), 0)[None, :]
    own = lax.dynamic_slice_in_dim(references, dom * SLAB, SLAB, 2).reshape(OWN, SLAB)
    vmem = pl.BlockSpec(memory_space=pltpu.VMEM)
    out = pl.pallas_call(
        kernel,
        out_shape=jax.ShapeDtypeStruct((OWN, SLAB), F32),
        in_specs=[pl.BlockSpec(memory_space=pl.ANY), vmem, vmem],
        out_specs=vmem,
        scratch_shapes=[
            pltpu.VMEM((CHUNKS, DOM, ROWS, WIDE), BF16),
            pltpu.VMEM((CLS, OWN, SLAB), BF16),
            pltpu.VMEM((DOM, 1, 128), jnp.int32),
            pltpu.VMEM((GROUPS, MEMBERS), BF16),
            pltpu.VMEM((MEMBERS, GROUPS), BF16),
            pltpu.VMEM((PANELS, MEMBERS), F32),
            pltpu.VMEM((PANELS, GROUPS), F32),
            pltpu.VMEM((DOM, 4, 128), F32),
            pltpu.VMEM((DOM, 4, 128), F32),
            pltpu.VMEM((DOM, 4, 128), F32),
            pltpu.VMEM((CLASSES, MEMBERS), F32),
            pltpu.VMEM((CLS, OWN, SLAB), BF16),
            pltpu.VMEM((CLS, OWN, SLAB), BF16),
            pltpu.VMEM((CLS, OWN, 128), F32),
            pltpu.VMEM((CLS, OWN, 128), F32),
            pltpu.SemaphoreType.DMA((CHUNKS,)),
            pltpu.SemaphoreType.DMA((6,)),
            pltpu.SemaphoreType.DMA((7,)),
            pltpu.SemaphoreType.DMA((CHUNKS,)),
        ],
        compiler_params=pltpu.CompilerParams(
            collective_id=0, has_side_effects=True, vmem_limit_bytes=48 * 1024 * 1024
        ),
    )(particles, own, codes)
    return out.reshape(CLASSES // CLS, BINS, SLAB)


def solution(mesh):
    in_specs = (
        P(("cls", "dom"), None),
        P("cls", None, None),
        P(("cls", "dom")),
        P(("cls", "dom"), None),
        P(("cls", "dom")),
    )
    out_specs = P("cls", None, "dom")
    return jax.shard_map(shards, mesh=mesh, in_specs=in_specs, out_specs=out_specs, check_vma=False)
```

time: 399 us -> 84.2 us (0.21); the launches traced: 395 us -> 84.1 us
  waiting for transfers between devices: 255 us -> 0 us
  blocking collectives: 92.4 us -> 0 us
  Pallas kernels: 0 us -> 80.5 us
  between operations: 14.2 us -> 0.01 us
  starting transfers between devices: 12.8 us -> 0 us
  matrix products: 10.6 us -> 0 us
  other arithmetic: 5.22 us -> 0.79 us
    psum x1 -> x0, waiting for transfers between devices: 238 us -> none  [shards(): scores = lax.psum(partial, 'dom') * (1.0 / math.sqrt(voxels))]
    pallas_call x0 -> x1, Pallas kernels: none -> 80.5 us  [shards(): pl.pallas_call(kernel, out_shape=jax.ShapeDtypeStruct((OWN, SLAB), F32),...]
    unnamed x1 -> x0, blocking collectives: 54.8 us -> none
    all_gather x1 -> x0, blocking collectives: 22.4 us -> none  [shards(): lax.all_gather(own, 'cls', axis=0, tiled=True)]
    reduce_scatter x1 -> x0, waiting for transfers between devices: 17 us -> none  [shards(): lax.psum_scatter(accumulated.reshape(classes, bins_all, slab), 'cls', sca...]
    psum x1 -> x0, blocking collectives: 15.2 us -> none  [shards(): totals = lax.psum(weight_sum, 'cls').reshape(classes, bins_all)]
    all_to_all x1 -> x0, starting transfers between devices: 12.7 us -> none  [shards(): lax.all_to_all(particles.reshape(rows, sources, slab), 'dom', split_axis=...]
    dot_general x6 -> x0, matrix products: 10.6 us -> none  [the longest x1 2.84 us: shards(): lax.dot_general(coefficient, whitened, (((0,), (0,)), ((), ())), preferre...]
  transfers between devices with their start and end apart: 3 -> 0, of which waited for: 2 -> 0; matrix products, arithmetic and copies ran while one was open for 0% -> 0% of each run, Pallas kernels for 0% -> 0%
where the time goes in v2:
time: 84.2 us; the launch traced here: 84.1 us
  Pallas kernels  80.5 us (96%)
  local copies, waits for them, and re-layouts  2.7 us (3%)
    pallas_call x1, Pallas kernels, shards(): pl.pallas_call(kernel, out_shape=jax.ShapeDtypeStruct((OWN, SLAB), F32),...  80.5 us
    unnamed x5, local copies, waits for them, and re-layouts  2.61 us

profile of v2, /device:TPU:1, one launch (start us, length us, event | category | flops | bytes accessed | tf_op | source)
XLA Modules:
  0.0 84.1 jit_solution(17948705886004421175)
XLA Ops:
  0.0 0.0 copy-start
  0.0 0.8 fusion.1
  0.8 0.1 tile.10
  0.9 0.4 copy-done
  1.3 0.0 copy-start.1
  1.3 1.6 %copy-done.1 = bf16[32,32768]{1,0:T(8,128)(2,1)S(1)} copy-done((bf16[32,32768]{1,0:T(8,128)(2,1)S(1)}, bf16[32,32768]{1,0:T(8,128)(2,1)}, u32[]{:S(2)}) %copy-start.1) | copy-done | bytes 2097176
  2.9 80.5 %shard_map.55 = f32[16,1024]{1,0:T(8,128)S(1)} custom-call(bf16[32,32768]{1,0:T(8,128)(2,1)S(1)} %copy-done.1, bf16[16,1024]{1,0:T(8,128)(2,1)S(1)} %dynamic-slice_bitcast_fusion.references, s32[1,128]{1,0:T(1,128)S(1)} %compare_select_fusion.codes), custom_call_target="tpu_custom_call" | custom-call | tf_op jit(solution)/shard_map/pallas_call | solution.py:281
  83.4 0.6 copy.7
  (3 shorter events, 0.0 us)
Async XLA Ops:
  0.0 1.3 %copy-start = (bf16[2,8,32768]{2,1,0:T(8,128)(2,1)S(1)}, bf16[2,8,32768]{2,1,0:T(8,128)(2,1)}, u32[]{:S(2)}) copy-start(bf16[2,8,32768]{2,1,0:T(8,128)(2,1)} %param.6) | copy-start | bytes 3145732
  1.3 1.6 %copy-start.1 = (bf16[32,32768]{1,0:T(8,128)(2,1)S(1)}, bf16[32,32768]{1,0:T(8,128)(2,1)}, u32[]{:S(2)}) copy-start(bf16[32,32768]{1,0:T(8,128)(2,1)} %particles.1) | copy-start | bytes 6291460

commit v3 on v2

--- a/solution.py
+++ b/solution.py
@@ -59,30 +59,56 @@
 def kernel(
     particles,
     references,
-    codes,
+    orient_bins,
+    destinations,
+    group_slots,
     out,
-    x_ref,
-    r_ref,
-    c_ref,
-    hot_t,
-    hot,
-    score_sum,
-    energy_sum,
-    piece_out,
-    piece_in,
-    piece_all,
-    scores_ref,
-    acc_out,
-    acc_in,
-    tot_out,
-    tot_in,
-    x_recv,
-    misc_recv,
-    send,
-    local,
+    *scratch,
 ):
+    (
+        x_ref,
+        labels,
+        codes,
+        r_ref,
+        c_ref,
+        hot_t,
+        hot,
+        score_sum,
+        energy_sum,
+        piece_out,
+        piece_in,
+        piece_all,
+        scores_ref,
+        coefficient_ref,
+        acc_out,
+        acc_in,
+        x_recv,
+        misc_recv,
+        send,
+        local,
+    ) = scratch
     cls = lax.axis_index("cls")
     dom = lax.axis_index("dom")
+    slab_start = pl.multiple_of(dom * SLAB, SLAB)
+
+    label_copies = [
+        pltpu.make_async_copy(ref, labels.at[k], local.at[k])
+        for k, ref in enumerate((destinations, group_slots, orient_bins))
+    ]
+    own_copies = [
+        pltpu.make_async_copy(references.at[:, pl.ds(slab_start, SLAB)], r_ref.at[cls], local.at[3])
+    ]
+    for chunk in range(CHUNKS):
+        start = pl.multiple_of(dom * SLAB + chunk * WIDE, WIDE)
+        own_copies.append(
+            pltpu.make_async_copy(
+                particles.at[:, pl.ds(start, WIDE)],
+                x_ref.at[chunk, dom],
+                local.at[4 + chunk],
+            )
+        )
+    for copy in label_copies + own_copies:
+        copy.start()
 
     barrier = pltpu.get_barrier_semaphore()
 
@@ -96,6 +122,15 @@
 
     lax.fori_loop(0, DOM - 1, greet_dom, 0)
     lax.fori_loop(1, CLS, greet_cls, 0)
+
+    for copy in label_copies:
+        copy.wait()
+    own_code = (labels[0] * 8 + labels[1]) * BINS + labels[2]
+    lane = lax.broadcasted_iota(jnp.int32, (1, 128), 1)
+    four = jnp.concatenate([own_code] * 4, axis=1)
+    codes[...] = jnp.where(lane // ROWS == dom % 4, four, 0)
+    c_ref[dom] = codes[...]
+
     pl.semaphore_wait(barrier, DOM - 1 + CLS - 1)
 
     def send_to(src, dst, sem_out, sem_in, device):
@@ -110,17 +145,6 @@
 
     def taken(ref, sem):
         pltpu.make_async_copy(ref, ref, sem).wait()
-
-    def send_codes(i, carry):
-        send_to(codes, c_ref.at[dom], send.at[0], misc_recv.at[0], (cls, dom_peer(i, dom)))
-        return carry
-
-    def send_panels(i, carry):
-        send_to(references, r_ref.at[cls], send.at[1], misc_recv.at[1], ((cls + i) % CLS, dom))
-        return carry
-
-    lax.fori_loop(0, DOM - 1, send_codes, 0)
-    lax.fori_loop(1, CLS, send_panels, 0)
 
     def send_chunk(k, carry):
         chunk, i = k // (DOM - 1), k % (DOM - 1)
@@ -135,20 +159,24 @@
         )
         return carry
 
-    lax.fori_loop(0, CHUNKS * (DOM - 1), send_chunk, 0)
-
-    own_copies = []
-    for chunk in range(CHUNKS):
-        start = pl.multiple_of(dom * SLAB + chunk * WIDE, WIDE)
-        own_copies.append(
-            pltpu.make_async_copy(
-                particles.at[:, pl.ds(start, WIDE)], x_ref.at[chunk, dom], local.at[chunk]
-            )
-        )
-    for copy in own_copies:
-        copy.start()
-    c_ref[dom] = codes[...]
-    r_ref[cls] = references[...]
+    def send_codes(i, carry):
+        send_to(codes, c_ref.at[dom], send.at[0], misc_recv.at[0], (cls, dom_peer(i, dom)))
+        return carry
+
+    def send_panels(i, carry):
+        send_to(
+            references.at[:, pl.ds(slab_start, SLAB)],
+            r_ref.at[cls],
+            send.at[1],
+            misc_recv.at[1],
+            ((cls + i) % CLS, dom),
+        )
+        return carry
+
+    lax.fori_loop(0, DOM - 1, send_chunk, 0)
+    lax.fori_loop(0, DOM - 1, send_codes, 0)
+    lax.fori_loop(1, CLS, send_panels, 0)
+    lax.fori_loop(DOM - 1, CHUNKS * (DOM - 1), send_chunk, 0)
 
     taken(c_ref.at[pl.ds(0, DOM - 1)], misc_recv.at[0])
     code = jnp.sum(c_ref[...].reshape(8, 4, 128), axis=1)
@@ -231,60 +259,56 @@
     power = jnp.exp(scores - jnp.max(scores, axis=0, keepdims=True))
     weights = (power / jnp.sum(power, axis=0, keepdims=True)).astype(BF16).astype(F32)
     coefficient_f32 = jnp.where(in_bin[None], weights[:, None, :], 0.0).reshape(PANELS, MEMBERS)
-    coefficient = coefficient_f32.astype(BF16)
+    coefficient_ref[...] = coefficient_f32.astype(BF16)
     totals = jnp.sum(coefficient_f32, axis=1, keepdims=True)
-    tot_out[...] = jnp.broadcast_to(totals, (PANELS, 128)).reshape(CLS, OWN, 128)
-
-    def send_total(i, carry):
-        peer = (cls + i) % CLS
-        send_to(tot_out.at[peer], tot_in.at[cls], send.at[5], misc_recv.at[4], (peer, dom))
-        return carry
-
-    lax.fori_loop(1, CLS, send_total, 0)
-    tot_in[cls] = tot_out[cls]
-
-    for chunk in range(CHUNKS):
-        acc_out[:, :, chunk * WIDE : (chunk + 1) * WIDE] = (
-            dot(coefficient, x_ref[chunk].reshape(MEMBERS, WIDE))
-            .astype(acc_out.dtype)
+    lane = lax.broadcasted_iota(jnp.int32, (PANELS, 128), 1)
+    tail = jnp.zeros((PANELS, 128), F32)
+    for k, piece in enumerate(split(totals, 3)):
+        tail = jnp.where(lane == k, piece.astype(F32), tail)
+    acc_out[:, :, SLAB:] = tail.astype(BF16).reshape(CLS, OWN, 128)
+    def add_up(chunk, carry):
+        lanes = pl.ds(pl.multiple_of(chunk * WIDE, WIDE), WIDE)
+        acc_out[:, :, lanes] = (
+            dot(coefficient_ref[...], x_ref[chunk].reshape(MEMBERS, WIDE))
+            .astype(BF16)
             .reshape(CLS, OWN, WIDE)
         )
+        return carry
+
+    lax.fori_loop(0, CHUNKS, add_up, 0)
 
     def send_acc(i, carry):
         peer = (cls + i) % CLS
-        send_to(acc_out.at[peer], acc_in.at[cls], send.at[6], misc_recv.at[5], (peer, dom))
+        send_to(acc_out.at[peer], acc_in.at[cls], send.at[5], misc_recv.at[4], (peer, dom))
         return carry
 
     lax.fori_loop(1, CLS, send_acc, 0)
     acc_in[cls] = acc_out[cls]
-    taken(tot_in.at[pl.ds(0, CLS - 1)], misc_recv.at[4])
-    total = jnp.sum(tot_in[...], axis=0)[:, 0:1]
-    taken(acc_in.at[pl.ds(0, CLS - 1)], misc_recv.at[5])
-    out[...] = jnp.sum(acc_in[...].astype(F32), axis=0) / (total + 1.0)
+    taken(acc_in.at[pl.ds(0, CLS - 1)], misc_recv.at[4])
+    total = jnp.sum(
+        jnp.sum(acc_in[:, :, SLAB:].astype(F32), axis=0), axis=1, keepdims=True
+    )
+    out[...] = jnp.sum(acc_in[:, :, :SLAB].astype(F32), axis=0) / (total + 1.0)
 
     taken(c_ref.at[pl.ds(0, DOM - 1)], send.at[0])
     taken(r_ref.at[pl.ds(0, CLS - 1)], send.at[1])
     taken(x_ref.at[:, pl.ds(0, DOM - 1)], send.at[2])
     taken(piece_in.at[pl.ds(0, DOM - 1)], send.at[3])
     taken(piece_all.at[pl.ds(0, DOM - 1)], send.at[4])
-    taken(tot_in.at[pl.ds(0, CLS - 1)], send.at[5])
-    taken(acc_in.at[pl.ds(0, CLS - 1)], send.at[6])
+    taken(acc_in.at[pl.ds(0, CLS - 1)], send.at[5])
 
 
 def shards(particles, references, orient_bins, destinations, group_slots):
-    dom = lax.axis_index("dom")
-    code = (destinations[:, 0] * 8 + group_slots) * BINS + orient_bins
-    lane = jnp.arange(128, dtype=jnp.int32)
-    codes = jnp.where(lane // ROWS == dom % 4, jnp.tile(code, 4), 0)[None, :]
-    own = lax.dynamic_slice_in_dim(references, dom * SLAB, SLAB, 2).reshape(OWN, SLAB)
-    vmem = pl.BlockSpec(memory_space=pltpu.VMEM)
+    hbm = pl.BlockSpec(memory_space=pltpu.HBM)
     out = pl.pallas_call(
         kernel,
         out_shape=jax.ShapeDtypeStruct((OWN, SLAB), F32),
-        in_specs=[pl.BlockSpec(memory_space=pl.ANY), vmem, vmem],
-        out_specs=vmem,
+        in_specs=[hbm] * 5,
+        out_specs=pl.BlockSpec(memory_space=pltpu.VMEM),
         scratch_shapes=[
             pltpu.VMEM((CHUNKS, DOM, ROWS, WIDE), BF16),
+            pltpu.VMEM((3, 1, ROWS), jnp.int32),
+            pltpu.VMEM((1, 128), jnp.int32),
             pltpu.VMEM((CLS, OWN, SLAB), BF16),
             pltpu.VMEM((DOM, 1, 128), jnp.int32),
             pltpu.VMEM((GROUPS, MEMBERS), BF16),
@@ -295,19 +319,24 @@
             pltpu.VMEM((DOM, 4, 128), F32),
             pltpu.VMEM((DOM, 4, 128), F32),
             pltpu.VMEM((CLASSES, MEMBERS), F32),
-            pltpu.VMEM((CLS, OWN, SLAB), BF16),
-            pltpu.VMEM((CLS, OWN, SLAB), BF16),
-            pltpu.VMEM((CLS, OWN, 128), F32),
-            pltpu.VMEM((CLS, OWN, 128), F32),
+            pltpu.VMEM((PANELS, MEMBERS), BF16),
+            pltpu.VMEM((CLS, OWN, SLAB + 128), BF16),
+            pltpu.VMEM((CLS, OWN, SLAB + 128), BF16),
             pltpu.SemaphoreType.DMA((CHUNKS,)),
+            pltpu.SemaphoreType.DMA((5,)),
             pltpu.SemaphoreType.DMA((6,)),
-            pltpu.SemaphoreType.DMA((7,)),
-            pltpu.SemaphoreType.DMA((CHUNKS,)),
+            pltpu.SemaphoreType.DMA((4 + CHUNKS,)),
         ],
         compiler_params=pltpu.CompilerParams(
-            collective_id=0, has_side_effects=True, vmem_limit_bytes=48 * 1024 * 1024
+            collective_id=0, has_side_effects=True, vmem_limit_bytes=60 * 1024 * 1024
         ),
-    )(particles, own, codes)
+    )(
+        particles,
+        references.reshape(OWN, DOM * SLAB),
+        orient_bins.reshape(1, ROWS),
+        destinations.reshape(1, ROWS),
+        group_slots.reshape(1, ROWS),
+    )
     return out.reshape(CLASSES // CLS, BINS, SLAB)
 
 

time: 84.2 us -> 81.8 us (0.971)
  local copies, waits for them, and re-layouts: 2.7 us -> 1.47 us
    unnamed x5 -> x1, local copies, waits for them, and re-layouts: 2.61 us -> 1.47 us
where the time goes in v3:
time: 81.8 us; the launch traced here: 81.7 us
  Pallas kernels  80.2 us (98%)
  local copies, waits for them, and re-layouts  1.47 us (2%)
    pallas_call x1, Pallas kernels, shards(): pl.pallas_call(kernel, out_shape=jax.ShapeDtypeStruct((OWN, SLAB), F32),...  80.2 us

profile of v3, /device:TPU:1, one launch (start us, length us, event | category | flops | bytes accessed | tf_op | source)
XLA Modules:
  0.0 81.7 jit_solution(17632886786026712256)
XLA Ops:
  0.0 80.2 %shard_map.55 = f32[16,1024]{1,0:T(8,128)} custom-call(bf16[32,32768]{1,0:T(8,128)(2,1)} %particles.1, bf16[16,32768]{1,0:T(8,128)(2,1)} %bitcast.5, s32[1,32]{1,0:T(1,128)} %bitcast.7, s32[1,32]{1,0:T(1,128)} %bitcast.8, s32[1,32]{1,0:T(1,128)} %bitcast.9), custom_call_target="tpu_custom_call" | custom-call | tf_op jit(solution)/shard_map/pallas_call | solution.py:303
  80.2 1.5 %copy.7 = f32[2,8,1024]{2,1,0:T(8,128)} copy(f32[2,8,1024]{2,1,0:T(8,128)} %bitcast.6) | data formatting | bytes 131072

commit v4 on v3

--- a/solution.py
+++ b/solution.py
@@ -20,8 +20,10 @@
 GROUPS = 256
 MEMBERS = ROWS * DOM
 SLAB = 1024
-CHUNKS = 4
-WIDE = SLAB // CHUNKS
+WIDTHS = (256, 256, 256, 128, 128)
+STARTS = tuple(sum(WIDTHS[:c]) for c in range(len(WIDTHS)))
+CHUNKS = len(WIDTHS)
+WIDE = 128
 PANELS = CLASSES * BINS
 OWN = PANELS // CLS
 Z = 8
@@ -98,15 +100,9 @@
     own_copies = [
         pltpu.make_async_copy(references.at[:, pl.ds(slab_start, SLAB)], r_ref.at[cls], local.at[3])
     ]
-    for chunk in range(CHUNKS):
-        start = pl.multiple_of(dom * SLAB + chunk * WIDE, WIDE)
-        own_copies.append(
-            pltpu.make_async_copy(
-                particles.at[:, pl.ds(start, WIDE)],
-                x_ref.at[chunk, dom],
-                local.at[4 + chunk],
-            )
-        )
+    own_copies.append(
+        pltpu.make_async_copy(particles.at[:, pl.ds(slab_start, SLAB)], x_ref.at[dom], local.at[4])
+    )
     for copy in label_copies + own_copies:
         copy.start()
 
@@ -146,18 +142,23 @@
     def taken(ref, sem):
         pltpu.make_async_copy(ref, ref, sem).wait()
 
-    def send_chunk(k, carry):
-        chunk, i = k // (DOM - 1), k % (DOM - 1)
-        peer = dom_peer(i, dom)
-        start = pl.multiple_of(peer * SLAB + chunk * WIDE, WIDE)
-        send_to(
-            particles.at[:, pl.ds(start, WIDE)],
-            x_ref.at[chunk, dom],
-            send.at[2],
-            x_recv.at[chunk],
-            (cls, peer),
-        )
-        return carry
+    def chunk_of(ref, chunk):
+        return ref.at[pl.ds(0, DOM - 1), :, pl.ds(STARTS[chunk], WIDTHS[chunk])]
+
+    def send_chunk(chunk):
+        def body(i, carry):
+            peer = dom_peer(i, dom)
+            start = pl.multiple_of(peer * SLAB + STARTS[chunk], 128)
+            send_to(
+                particles.at[:, pl.ds(start, WIDTHS[chunk])],
+                x_ref.at[dom, :, pl.ds(STARTS[chunk], WIDTHS[chunk])],
+                send.at[2],
+                x_recv.at[chunk],
+                (cls, peer),
+            )
+            return carry
+
+        lax.fori_loop(0, DOM - 1, body, 0)
 
     def send_codes(i, carry):
         send_to(codes, c_ref.at[dom], send.at[0], misc_recv.at[0], (cls, dom_peer(i, dom)))
@@ -173,10 +174,11 @@
         )
         return carry
 
-    lax.fori_loop(0, DOM - 1, send_chunk, 0)
+    send_chunk(0)
     lax.fori_loop(0, DOM - 1, send_codes, 0)
     lax.fori_loop(1, CLS, send_panels, 0)
-    lax.fori_loop(DOM - 1, CHUNKS * (DOM - 1), send_chunk, 0)
+    for chunk in range(1, CHUNKS):
+        send_chunk(chunk)
 
     taken(c_ref.at[pl.ds(0, DOM - 1)], misc_recv.at[0])
     code = jnp.sum(c_ref[...].reshape(8, 4, 128), axis=1)
@@ -200,28 +202,30 @@
     for copy in own_copies:
         copy.wait()
 
-    def whiten(chunk, carry):
-        taken(x_ref.at[chunk, pl.ds(0, DOM - 1)], x_recv.at[chunk])
-        values = x_ref[chunk].reshape(MEMBERS, WIDE).astype(F32)
-        high, low = split(values * values, 2)
-        power = dot(hot_t[...], high) + dot(hot_t[...], low)
-        inverse = (counts + 1.0) / (power + 1.0)
+    def whiten(part, carry):
+        for chunk in range(CHUNKS):
+
+            @pl.when(part == STARTS[chunk] // WIDE)
+            def _():
+                taken(chunk_of(x_ref, chunk), x_recv.at[chunk])
+
+        lanes = pl.ds(pl.multiple_of(part * WIDE, WIDE), WIDE)
+        values = x_ref[:, :, lanes].reshape(MEMBERS, WIDE).astype(F32)
+        power = dot(hot_t[...], jnp.concatenate(split(values * values, 2), axis=1))
+        inverse = (counts + 1.0) / (power[:, :WIDE] + power[:, WIDE:] + 1.0)
         parts = split(inverse, 3)
-        spread = dot(hot[...], parts[0]) + dot(hot[...], parts[1])
-        whitened = (values * spread).astype(BF16)
-        x_ref[chunk] = whitened.reshape(DOM, ROWS, WIDE)
-        panels = r_ref[:, :, pl.ds(pl.multiple_of(chunk * WIDE, WIDE), WIDE)].reshape(PANELS, WIDE)
+        spread = dot(hot[...], jnp.concatenate(parts[:2], axis=1))
+        whitened = (values * (spread[:, :WIDE] + spread[:, WIDE:])).astype(BF16)
+        x_ref[:, :, lanes] = whitened.reshape(DOM, ROWS, WIDE)
+        panels = r_ref[:, :, lanes].reshape(PANELS, WIDE)
         score_sum[...] += dot_nt(panels, whitened)
         wide = panels.astype(F32)
-        square = split(wide * wide, 2)
-        energy = jnp.zeros((PANELS, GROUPS), F32)
-        for piece in square:
-            for part in parts:
-                energy += dot_nt(piece, part)
-        energy_sum[...] += energy
-        return carry
-
-    lax.fori_loop(0, CHUNKS, whiten, 0)
+        high, low = split(wide * wide, 2)
+        squares = jnp.concatenate([high, high, high, low, low, low], axis=1)
+        energy_sum[...] += dot_nt(squares, jnp.concatenate(parts + parts, axis=1))
+        return carry
+
+    lax.fori_loop(0, SLAB // WIDE, whiten, 0)
 
     spread_energy = jnp.zeros((PANELS, MEMBERS), F32)
     for part in split(energy_sum[...], 3):
@@ -266,16 +270,13 @@
     for k, piece in enumerate(split(totals, 3)):
         tail = jnp.where(lane == k, piece.astype(F32), tail)
     acc_out[:, :, SLAB:] = tail.astype(BF16).reshape(CLS, OWN, 128)
-    def add_up(chunk, carry):
-        lanes = pl.ds(pl.multiple_of(chunk * WIDE, WIDE), WIDE)
+    for half in range(4):
+        lanes = slice(half * 256, half * 256 + 256)
         acc_out[:, :, lanes] = (
-            dot(coefficient_ref[...], x_ref[chunk].reshape(MEMBERS, WIDE))
+            dot(coefficient_ref[...], x_ref[:, :, lanes].reshape(MEMBERS, 256))
             .astype(BF16)
-            .reshape(CLS, OWN, WIDE)
+            .reshape(CLS, OWN, 256)
         )
-        return carry
-
-    lax.fori_loop(0, CHUNKS, add_up, 0)
 
     def send_acc(i, carry):
         peer = (cls + i) % CLS
@@ -292,7 +293,7 @@
 
     taken(c_ref.at[pl.ds(0, DOM - 1)], send.at[0])
     taken(r_ref.at[pl.ds(0, CLS - 1)], send.at[1])
-    taken(x_ref.at[:, pl.ds(0, DOM - 1)], send.at[2])
+    taken(x_ref.at[pl.ds(0, DOM - 1)], send.at[2])
     taken(piece_in.at[pl.ds(0, DOM - 1)], send.at[3])
     taken(piece_all.at[pl.ds(0, DOM - 1)], send.at[4])
     taken(acc_in.at[pl.ds(0, CLS - 1)], send.at[5])
@@ -306,7 +307,7 @@
         in_specs=[hbm] * 5,
         out_specs=pl.BlockSpec(memory_space=pltpu.VMEM),
         scratch_shapes=[
-            pltpu.VMEM((CHUNKS, DOM, ROWS, WIDE), BF16),
+            pltpu.VMEM((DOM, ROWS, SLAB), BF16),
             pltpu.VMEM((3, 1, ROWS), jnp.int32),
             pltpu.VMEM((1, 128), jnp.int32),
             pltpu.VMEM((CLS, OWN, SLAB), BF16),
@@ -325,17 +326,22 @@
             pltpu.SemaphoreType.DMA((CHUNKS,)),
             pltpu.SemaphoreType.DMA((5,)),
             pltpu.SemaphoreType.DMA((6,)),
-            pltpu.SemaphoreType.DMA((4 + CHUNKS,)),
+            pltpu.SemaphoreType.DMA((5,)),
         ],
         compiler_params=pltpu.CompilerParams(
-            collective_id=0, has_side_effects=True, vmem_limit_bytes=60 * 1024 * 1024
+            collective_id=0, has_side_effects=True, vmem_limit_bytes=48 * 1024 * 1024
         ),
     )(
-        particles,
-        references.reshape(OWN, DOM * SLAB),
-        orient_bins.reshape(1, ROWS),
-        destinations.reshape(1, ROWS),
-        group_slots.reshape(1, ROWS),
+        *(
+            pltpu.with_memory_space_constraint(value, pltpu.HBM)
+            for value in (
+                particles,
+                references.reshape(OWN, DOM * SLAB),
+                orient_bins.reshape(1, ROWS),
+                destinations.reshape(1, ROWS),
+                group_slots.reshape(1, ROWS),
+            )
+        )
     )
     return out.reshape(CLASSES // CLS, BINS, SLAB)
 

time: 81.8 us -> 78.8 us (0.963)
  Pallas kernels: 80.2 us -> 77.9 us
  local copies, waits for them, and re-layouts: 1.47 us -> 0.63 us
    pallas_call x1, Pallas kernels: 80.2 us -> 77.9 us  [shards(): pl.pallas_call(kernel, out_shape=jax.ShapeDtypeStruct((OWN, SLAB), F32),...]
    unnamed x1, local copies, waits for them, and re-layouts: 1.47 us -> 0.63 us
where the time goes in v4:
time: 78.8 us; the launch traced here: 78.5 us
  Pallas kernels  77.9 us (99%)
    pallas_call x1, Pallas kernels, shards(): pl.pallas_call(kernel, out_shape=jax.ShapeDtypeStruct((OWN, SLAB), F32),...  77.9 us

profile of v4, /device:TPU:1, one launch (start us, length us, event | category | flops | bytes accessed | tf_op | source)
XLA Modules:
  0.0 78.5 jit_solution(11940293925149050537)
XLA Ops:
  0.0 77.9 %shard_map.55 = f32[16,1024]{1,0:T(8,128)S(1)} custom-call(bf16[32,32768]{1,0:T(8,128)(2,1)} %particles.1, bf16[16,32768]{1,0:T(8,128)(2,1)} %bitcast.6, s32[1,32]{1,0:T(1,128)} %bitcast.7, s32[1,32]{1,0:T(1,128)} %bitcast.8, s32[1,32]{1,0:T(1,128)} %bitcast.9), custom_call_target="tpu_custom_call" | custom-call | tf_op jit(solution)/shard_map/pallas_call | solution.py:304
  77.9 0.6 copy.7

commit v5 on v4

--- a/solution.py
+++ b/solution.py
@@ -27,6 +27,8 @@
 PANELS = CLASSES * BINS
 OWN = PANELS // CLS
 Z = 8
+Y = 4
+STEPS = ((1, 2), (1, 1), (1, 3), (1, 0), (0, 2), (0, 1), (0, 3))
 
 NT = (((1,), (1,)), ((), ()))
 
@@ -69,6 +71,7 @@
 ):
     (
         x_ref,
+        rows,
         labels,
         codes,
         r_ref,
@@ -82,6 +85,9 @@
         piece_all,
         scores_ref,
         coefficient_ref,
+        tot_out,
+        tot_in,
+        tot_col,
         acc_out,
         acc_in,
         x_recv,
@@ -91,6 +97,20 @@
     ) = scratch
     cls = lax.axis_index("cls")
     dom = lax.axis_index("dom")
+
+    barrier = pltpu.get_barrier_semaphore()
+
+    def greet_dom(i, carry):
+        pl.semaphore_signal(barrier, inc=1, device_id=(cls, dom_peer(i, dom)), device_id_type=MESH)
+        return carry
+
+    def greet_cls(i, carry):
+        pl.semaphore_signal(barrier, inc=1, device_id=((cls + i) % CLS, dom), device_id_type=MESH)
+        return carry
+
+    lax.fori_loop(0, DOM - 1, greet_dom, 0)
+    lax.fori_loop(1, CLS, greet_cls, 0)
+
     slab_start = pl.multiple_of(dom * SLAB, SLAB)
 
     label_copies = [
@@ -100,24 +120,9 @@
     own_copies = [
         pltpu.make_async_copy(references.at[:, pl.ds(slab_start, SLAB)], r_ref.at[cls], local.at[3])
     ]
-    own_copies.append(
-        pltpu.make_async_copy(particles.at[:, pl.ds(slab_start, SLAB)], x_ref.at[dom], local.at[4])
-    )
-    for copy in label_copies + own_copies:
+    staged = pltpu.make_async_copy(particles, rows, local.at[4])
+    for copy in label_copies + own_copies + [staged]:
         copy.start()
-
-    barrier = pltpu.get_barrier_semaphore()
-
-    def greet_dom(i, carry):
-        pl.semaphore_signal(barrier, inc=1, device_id=(cls, dom_peer(i, dom)), device_id_type=MESH)
-        return carry
-
-    def greet_cls(i, carry):
-        pl.semaphore_signal(barrier, inc=1, device_id=((cls + i) % CLS, dom), device_id_type=MESH)
-        return carry
-
-    lax.fori_loop(0, DOM - 1, greet_dom, 0)
-    lax.fori_loop(1, CLS, greet_cls, 0)
 
     for copy in label_copies:
         copy.wait()
@@ -127,6 +132,8 @@
     codes[...] = jnp.where(lane // ROWS == dom % 4, four, 0)
     c_ref[dom] = codes[...]
 
+    staged.wait()
+    x_ref[dom] = rows[:, pl.ds(slab_start, SLAB)]
     pl.semaphore_wait(barrier, DOM - 1 + CLS - 1)
 
     def send_to(src, dst, sem_out, sem_in, device):
@@ -150,7 +157,7 @@
             peer = dom_peer(i, dom)
             start = pl.multiple_of(peer * SLAB + STARTS[chunk], 128)
             send_to(
-                particles.at[:, pl.ds(start, WIDTHS[chunk])],
+                rows.at[:, pl.ds(start, WIDTHS[chunk])],
                 x_ref.at[dom, :, pl.ds(STARTS[chunk], WIDTHS[chunk])],
                 send.at[2],
                 x_recv.at[chunk],
@@ -264,32 +271,28 @@
     weights = (power / jnp.sum(power, axis=0, keepdims=True)).astype(BF16).astype(F32)
     coefficient_f32 = jnp.where(in_bin[None], weights[:, None, :], 0.0).reshape(PANELS, MEMBERS)
     coefficient_ref[...] = coefficient_f32.astype(BF16)
-    totals = jnp.sum(coefficient_f32, axis=1, keepdims=True)
-    lane = lax.broadcasted_iota(jnp.int32, (PANELS, 128), 1)
-    tail = jnp.zeros((PANELS, 128), F32)
-    for k, piece in enumerate(split(totals, 3)):
-        tail = jnp.where(lane == k, piece.astype(F32), tail)
-    acc_out[:, :, SLAB:] = tail.astype(BF16).reshape(CLS, OWN, 128)
-    for half in range(4):
-        lanes = slice(half * 256, half * 256 + 256)
-        acc_out[:, :, lanes] = (
-            dot(coefficient_ref[...], x_ref[:, :, lanes].reshape(MEMBERS, 256))
+    tot_out[...] = dot_nt(jnp.ones((16, MEMBERS), BF16), coefficient_ref[...])[0:1]
+
+    peers = [((cls // Y + dx) % 2) * Y + (cls + dy) % Y for dx, dy in STEPS]
+    for peer in peers:
+        send_to(tot_out, tot_in.at[cls], send.at[6], misc_recv.at[5], (peer, dom))
+    tot_in[cls] = tot_out[...]
+    for start in range(0, SLAB, 256):
+        acc_out[:, :, start : start + 256] = (
+            dot(coefficient_ref[...], x_ref[:, :, start : start + 256].reshape(MEMBERS, 256))
             .astype(BF16)
             .reshape(CLS, OWN, 256)
         )
-
-    def send_acc(i, carry):
-        peer = (cls + i) % CLS
+    for peer in peers:
         send_to(acc_out.at[peer], acc_in.at[cls], send.at[5], misc_recv.at[4], (peer, dom))
-        return carry
-
-    lax.fori_loop(1, CLS, send_acc, 0)
     acc_in[cls] = acc_out[cls]
+
+    taken(tot_in.at[pl.ds(0, CLS - 1)], misc_recv.at[5])
+    total = jnp.sum(tot_in[...], axis=0)
+    tot_col[...] = jnp.transpose(jnp.broadcast_to(total, (PANELS, 128)))
+    own_total = tot_col[pl.ds(pl.multiple_of(cls * OWN, OWN), OWN), 0:1]
     taken(acc_in.at[pl.ds(0, CLS - 1)], misc_recv.at[4])
-    total = jnp.sum(
-        jnp.sum(acc_in[:, :, SLAB:].astype(F32), axis=0), axis=1, keepdims=True
-    )
-    out[...] = jnp.sum(acc_in[:, :, :SLAB].astype(F32), axis=0) / (total + 1.0)
+    out[...] = jnp.sum(acc_in[...].astype(F32), axis=0) / (own_total + 1.0)
 
     taken(c_ref.at[pl.ds(0, DOM - 1)], send.at[0])
     taken(r_ref.at[pl.ds(0, CLS - 1)], send.at[1])
@@ -297,6 +300,7 @@
     taken(piece_in.at[pl.ds(0, DOM - 1)], send.at[3])
     taken(piece_all.at[pl.ds(0, DOM - 1)], send.at[4])
     taken(acc_in.at[pl.ds(0, CLS - 1)], send.at[5])
+    taken(tot_in.at[pl.ds(0, CLS - 1)], send.at[6])
 
 
 def shards(particles, references, orient_bins, destinations, group_slots):
@@ -308,6 +312,7 @@
         out_specs=pl.BlockSpec(memory_space=pltpu.VMEM),
         scratch_shapes=[
             pltpu.VMEM((DOM, ROWS, SLAB), BF16),
+            pltpu.VMEM((ROWS, DOM * SLAB), BF16),
             pltpu.VMEM((3, 1, ROWS), jnp.int32),
             pltpu.VMEM((1, 128), jnp.int32),
             pltpu.VMEM((CLS, OWN, SLAB), BF16),
@@ -321,11 +326,14 @@
             pltpu.VMEM((DOM, 4, 128), F32),
             pltpu.VMEM((CLASSES, MEMBERS), F32),
             pltpu.VMEM((PANELS, MEMBERS), BF16),
-            pltpu.VMEM((CLS, OWN, SLAB + 128), BF16),
-            pltpu.VMEM((CLS, OWN, SLAB + 128), BF16),
+            pltpu.VMEM((1, PANELS), F32),
+            pltpu.VMEM((CLS, 1, PANELS), F32),
+            pltpu.VMEM((PANELS, 128), F32),
+            pltpu.VMEM((CLS, OWN, SLAB), BF16),
+            pltpu.VMEM((CLS, OWN, SLAB), BF16),
             pltpu.SemaphoreType.DMA((CHUNKS,)),
-            pltpu.SemaphoreType.DMA((5,)),
             pltpu.SemaphoreType.DMA((6,)),
+            pltpu.SemaphoreType.DMA((7,)),
             pltpu.SemaphoreType.DMA((5,)),
         ],
         compiler_params=pltpu.CompilerParams(

time: 78.8 us -> 78.6 us (level)
  no operation moved by 1% of the time
where the time goes in v5:
time: 78.6 us; the launch traced here: 78.5 us
  Pallas kernels  77.8 us (99%)
    pallas_call x1, Pallas kernels, shards(): pl.pallas_call(kernel, out_shape=jax.ShapeDtypeStruct((OWN, SLAB), F32),...  77.8 us

profile of v5, /device:TPU:1, one launch (start us, length us, event | category | flops | bytes accessed | tf_op | source)
XLA Modules:
  0.0 78.5 jit_solution(13660355047945573973)
XLA Ops:
  0.0 77.8 %shard_map.55 = f32[16,1024]{1,0:T(8,128)S(1)} custom-call(bf16[32,32768]{1,0:T(8,128)(2,1)} %particles.1, bf16[16,32768]{1,0:T(8,128)(2,1)} %bitcast.6, s32[1,32]{1,0:T(1,128)} %bitcast.7, s32[1,32]{1,0:T(1,128)} %bitcast.8, s32[1,32]{1,0:T(1,128)} %bitcast.9), custom_call_target="tpu_custom_call" | custom-call | tf_op jit(solution)/shard_map/pallas_call | solution.py:308
  77.8 0.6 copy.7

commit v6 on v5

--- a/solution.py
+++ b/solution.py
@@ -20,7 +20,7 @@
 GROUPS = 256
 MEMBERS = ROWS * DOM
 SLAB = 1024
-WIDTHS = (256, 256, 256, 128, 128)
+WIDTHS = (512, 384, 128)
 STARTS = tuple(sum(WIDTHS[:c]) for c in range(len(WIDTHS)))
 CHUNKS = len(WIDTHS)
 WIDE = 128

time: 78.6 us -> 78.4 us (level)
  no operation moved by 1% of the time
where the time goes in v6:
time: 78.4 us; the launch traced here: 78.1 us
  Pallas kernels  77.5 us (99%)
    pallas_call x1, Pallas kernels, shards(): pl.pallas_call(kernel, out_shape=jax.ShapeDtypeStruct((OWN, SLAB), F32),...  77.5 us

profile of v6, /device:TPU:1, one launch (start us, length us, event | category | flops | bytes accessed | tf_op | source)
XLA Modules:
  0.0 78.1 jit_solution(7496127971984038001)
XLA Ops:
  0.0 77.5 %shard_map.55 = f32[16,1024]{1,0:T(8,128)S(1)} custom-call(bf16[32,32768]{1,0:T(8,128)(2,1)} %particles.1, bf16[16,32768]{1,0:T(8,128)(2,1)} %bitcast.6, s32[1,32]{1,0:T(1,128)} %bitcast.7, s32[1,32]{1,0:T(1,128)} %bitcast.8, s32[1,32]{1,0:T(1,128)} %bitcast.9), custom_call_target="tpu_custom_call" | custom-call | tf_op jit(solution)/shard_map/pallas_call | solution.py:308
  77.5 0.6 copy.7

commit v7 on v6

--- a/solution.py
+++ b/solution.py
@@ -108,7 +108,8 @@
         pl.semaphore_signal(barrier, inc=1, device_id=((cls + i) % CLS, dom), device_id_type=MESH)
         return carry
 
-    lax.fori_loop(0, DOM - 1, greet_dom, 0)
+    for i in range(DOM - 1):
+        greet_dom(i, 0)
     lax.fori_loop(1, CLS, greet_cls, 0)
 
     slab_start = pl.multiple_of(dom * SLAB, SLAB)
@@ -250,7 +251,8 @@
         send_to(piece_out.at[peer], piece_in.at[dom], send.at[3], misc_recv.at[2], (cls, peer))
         return carry
 
-    lax.fori_loop(0, DOM - 1, send_piece, 0)
+    for i in range(DOM - 1):
+        send_piece(i, 0)
     piece_in[dom] = piece_out[dom]
     taken(piece_in.at[pl.ds(0, DOM - 1)], misc_recv.at[2])
     piece_all[dom] = jnp.sum(piece_in[...], axis=0)
@@ -260,7 +262,8 @@
         send_to(piece_all.at[dom], piece_all.at[dom], send.at[4], misc_recv.at[3], (cls, peer))
         return carry
 
-    lax.fori_loop(0, DOM - 1, send_sum, 0)
+    for i in range(DOM - 1):
+        send_sum(i, 0)
     taken(piece_all.at[pl.ds(0, DOM - 1)], misc_recv.at[3])
     for q in range(4):
         for t in range(8):

time: 78.4 us -> 78.2 us (level)
  no operation moved by 1% of the time
where the time goes in v7:
time: 78.2 us; the launch traced here: 77.8 us
  Pallas kernels  77.2 us (99%)
    pallas_call x1, Pallas kernels, shards(): pl.pallas_call(kernel, out_shape=jax.ShapeDtypeStruct((OWN, SLAB), F32),...  77.2 us

profile of v7, /device:TPU:1, one launch (start us, length us, event | category | flops | bytes accessed | tf_op | source)
XLA Modules:
  0.0 77.8 jit_solution(7435647476201921631)
XLA Ops:
  0.0 77.2 %shard_map.55 = f32[16,1024]{1,0:T(8,128)S(1)} custom-call(bf16[32,32768]{1,0:T(8,128)(2,1)} %particles.1, bf16[16,32768]{1,0:T(8,128)(2,1)} %bitcast.6, s32[1,32]{1,0:T(1,128)} %bitcast.7, s32[1,32]{1,0:T(1,128)} %bitcast.8, s32[1,32]{1,0:T(1,128)} %bitcast.9), custom_call_target="tpu_custom_call" | custom-call | tf_op jit(solution)/shard_map/pallas_call | solution.py:311
  77.2 0.6 copy.7

commit v8 on v7

--- a/solution.py
+++ b/solution.py
@@ -166,7 +166,8 @@
             )
             return carry
 
-        lax.fori_loop(0, DOM - 1, body, 0)
+        for i in range(DOM - 1):
+            body(i, 0)
 
     def send_codes(i, carry):
         send_to(codes, c_ref.at[dom], send.at[0], misc_recv.at[0], (cls, dom_peer(i, dom)))

time: 78.2 us -> 78.2 us (level)
  no operation moved by 1% of the time
where the time goes in v8:
time: 78.2 us; the launch traced here: 77.8 us
  Pallas kernels  77.2 us (99%)
    pallas_call x1, Pallas kernels, shards(): pl.pallas_call(kernel, out_shape=jax.ShapeDtypeStruct((OWN, SLAB), F32),...  77.2 us

profile of v8, /device:TPU:1, one launch (start us, length us, event | category | flops | bytes accessed | tf_op | source)
XLA Modules:
  0.0 77.8 jit_solution(1397770401154265552)
XLA Ops:
  0.0 77.2 %shard_map.55 = f32[16,1024]{1,0:T(8,128)S(1)} custom-call(bf16[32,32768]{1,0:T(8,128)(2,1)} %particles.1, bf16[16,32768]{1,0:T(8,128)(2,1)} %bitcast.6, s32[1,32]{1,0:T(1,128)} %bitcast.7, s32[1,32]{1,0:T(1,128)} %bitcast.8, s32[1,32]{1,0:T(1,128)} %bitcast.9), custom_call_target="tpu_custom_call" | custom-call | tf_op jit(solution)/shard_map/pallas_call | solution.py:312
  77.2 0.6 copy.7
